TPU v7x, 32 devices: a whole 2x2x4 slice. The times are simulated.
32 devices in a mesh: ctx: 4 (over y, x), head: 8 (over z, core).
Axes of the slice: x: 2, y: 2, z: 4, core: 2. Of those that a mesh axis runs over, the one named last changes fastest.
Arguments:
- queries: bfloat16 [32, 96, 4096], P(None, None, ('ctx', 'head')), may hold values from -9 to 9
- keys: bfloat16 [32, 96, 4096], P(None, None, ('ctx', 'head')), may hold values from -9 to 9
- values: bfloat16 [32, 96, 4096], P(None, None, ('ctx', 'head')), may hold values from -6 to 6
- doc_start: int32 [4096], P(('ctx', 'head')), may hold values from 0 to 4095, as said below
Outputs:
- grad_queries: bfloat16 [32, 96, 4096], P(None, None, ('ctx', 'head'))
- grad_keys: bfloat16 [32, 96, 4096], P(None, None, ('ctx', 'head'))
- grad_values: bfloat16 [32, 96, 4096], P(None, None, ('ctx', 'head'))
Inputs may be any that keep to these rules, and one draw needn't show every extreme that they name: doc_start never falls; doc_start[t] is t or doc_start[t-1], t - doc_start[t] < 512, the first document has exactly 512 positions, and at every multiple k of 1024 after 0 a document starts at k - 256 and runs through k + 512 // 2 - 1.
All inputs are finite; a program needn't handle non-finite values.
Results may differ from a plain program's by a relative error of at most 0.02.
Values may be sent and summed in bfloat16 or wider, within the bound.
A program may use at most 128 MiB of HBM per device.

v0:
```python
import math

import jax
import jax.numpy as jnp
from jax import lax
from jax.sharding import PartitionSpec as P

DOC_MAX = 512


def from_behind(value, axis, steps):
    count = lax.axis_size(axis)
    first, last = (max(0, -steps), min(count, count - steps))
    return lax.ppermute(value, axis, [(source, source + steps) for source in range(first, last)])


def block_grads(query_blk, key_win, value_win, first_pos, query_pos, key_pos, score_scale):
    visible = (key_pos[None, :] >= first_pos[:, None]) & (key_pos[None, :] <= query_pos[:, None])
    scores = (
        jnp.einsum("hdq,hdk->hqk", query_blk, key_win, preferred_element_type=jnp.float32)
        * score_scale
    )
    scores = jnp.where(visible[None], scores, -jnp.inf)
    row_peak = jnp.max(scores, axis=2, keepdims=True)
    weights = jnp.exp(scores - row_peak)
    soft_probs = weights / jnp.sum(weights, axis=2, keepdims=True)
    probs_low = soft_probs.astype(jnp.bfloat16)
    attended = jnp.einsum(
        "hqk,hdk->hdq", probs_low, value_win, preferred_element_type=jnp.float32
    ).astype(jnp.bfloat16)
    grad_value = jnp.einsum("hqk,hdq->hdk", probs_low, attended, preferred_element_type=jnp.float32)
    grad_probs = jnp.einsum("hdq,hdk->hqk", attended, value_win, preferred_element_type=jnp.float32)
    wide_att = attended.astype(jnp.float32)
    row_dot = jnp.sum(wide_att * wide_att, axis=1)
    grad_scores = (soft_probs * (grad_probs - row_dot[:, :, None])).astype(jnp.bfloat16)
    grad_query = (
        jnp.einsum("hqk,hdk->hdq", grad_scores, key_win, preferred_element_type=jnp.float32)
        * score_scale
    ).astype(jnp.bfloat16)
    grad_key = jnp.einsum(
        "hqk,hdq->hdk", grad_scores, query_blk, preferred_element_type=jnp.float32
    )
    return (grad_query, grad_key, grad_value)


def shards(queries, keys, values, doc_start):
    score_scale = 1.0 / math.sqrt(queries.shape[1])
    head_q, head_k, head_v = (
        lax.all_to_all(queries, "head", split_axis=0, concat_axis=2, tiled=True),
        lax.all_to_all(keys, "head", split_axis=0, concat_axis=2, tiled=True),
        lax.all_to_all(values, "head", split_axis=0, concat_axis=2, tiled=True),
    )
    starts = lax.all_gather(doc_start, "head", axis=0, tiled=True)
    local_heads = head_q.shape[0]
    head_depth = head_q.shape[1]
    group_span = head_q.shape[2]
    window = DOC_MAX
    blocks = group_span // window
    prior_k, prior_v = from_behind(
        (head_k[:, :, group_span - window :], head_v[:, :, group_span - window :]), "ctx", 1
    )
    anchor = lax.axis_index("ctx") * group_span
    key_ext = jnp.concatenate([prior_k, head_k], axis=2).reshape(
        local_heads, head_depth, blocks + 1, window
    )
    value_ext = jnp.concatenate([prior_v, head_v], axis=2).reshape(
        local_heads, head_depth, blocks + 1, window
    )
    key_wins = jnp.moveaxis(jnp.concatenate([key_ext[:, :, :-1], key_ext[:, :, 1:]], axis=3), 2, 0)
    value_wins = jnp.moveaxis(
        jnp.concatenate([value_ext[:, :, :-1], value_ext[:, :, 1:]], axis=3), 2, 0
    )
    query_blocks = jnp.moveaxis(head_q.reshape(local_heads, head_depth, blocks, window), 2, 0)
    start_blocks = starts.reshape(blocks, window)
    offsets = jnp.arange(window, dtype=jnp.int32)
    spread = jnp.arange(2 * window, dtype=jnp.int32)

    def one_block(unused_carry, block_item):
        query_blk, key_win, value_win, first_pos, number = block_item
        block_base = anchor + number * window
        query_pos = block_base + offsets
        key_pos = block_base - window + spread
        return (
            unused_carry,
            block_grads(query_blk, key_win, value_win, first_pos, query_pos, key_pos, score_scale),
        )

    _, (query_stack, key_stack, value_stack) = lax.scan(
        one_block,
        jnp.int32(0),
        (query_blocks, key_wins, value_wins, start_blocks, jnp.arange(blocks, dtype=jnp.int32)),
    )
    far_k = key_stack[..., :window]
    far_v = value_stack[..., :window]
    own_k = key_stack[..., window:] + jnp.concatenate(
        [far_k[1:], jnp.zeros_like(far_k[:1])], axis=0
    )
    own_v = value_stack[..., window:] + jnp.concatenate(
        [far_v[1:], jnp.zeros_like(far_v[:1])], axis=0
    )
    back_k, back_v = from_behind((far_k[0], far_v[0]), "ctx", -1)
    own_k = own_k.at[blocks - 1].add(back_k)
    own_v = own_v.at[blocks - 1].add(back_v)

    def to_span(stacked):
        return jnp.moveaxis(stacked, 0, 2).reshape(local_heads, head_depth, group_span)

    grad_q = to_span(query_stack)
    grad_k = (to_span(own_k) * score_scale).astype(jnp.bfloat16)
    grad_v = to_span(own_v).astype(jnp.bfloat16)
    return (
        lax.all_to_all(grad_q, "head", split_axis=2, concat_axis=0, tiled=True),
        lax.all_to_all(grad_k, "head", split_axis=2, concat_axis=0, tiled=True),
        lax.all_to_all(grad_v, "head", split_axis=2, concat_axis=0, tiled=True),
    )


def solution(mesh):
    return jax.shard_map(
        shards,
        mesh=mesh,
        in_specs=(
            P(None, None, ("ctx", "head")),
            P(None, None, ("ctx", "head")),
            P(None, None, ("ctx", "head")),
            P(("ctx", "head")),
        ),
        out_specs=(
            P(None, None, ("ctx", "head")),
            P(None, None, ("ctx", "head")),
            P(None, None, ("ctx", "head")),
        ),
        check_vma=False,
    )
```

profile of v0, /device:TPU:1, one launch (start us, length us, event | category | flops | bytes accessed | tf_op | source)
XLA Modules:
  0.0 246.2 jit_solution(4831469241479927829)
XLA Ops:
  0.6 26.3 %all_to_all.105 = bf16[32,96,128]{2,1,0:T(8,128)(2,1)S(1)} all-to-all(bf16[32,96,128]{2,1,0:T(8,128)(2,1)} %param.12), channel_id=1, replica_groups=mesh['ctx'=4,'head'=8] {'head'}, dimensions={0} | all-to-all | bytes 1572864 | tf_op jit(solution)/shard_map/all_to_all | solution.py:51
  27.0 24.4 %all_to_all.106 = bf16[32,96,128]{2,1,0:T(8,128)(2,1)S(1)} all-to-all(bf16[32,96,128]{2,1,0:T(8,128)(2,1)} %param.11), channel_id=1, replica_groups=mesh['ctx'=4,'head'=8] {'head'}, dimensions={0} | all-to-all | bytes 1572864 | tf_op jit(solution)/shard_map/all_to_all | solution.py:50
  51.4 4.5 %all-to-all-start.1 = ((bf16[32,96,128]{2,1,0:T(8,128)(2,1)}), bf16[32,96,128]{2,1,0:T(8,128)(2,1)S(1)}, u32[]{:S(2)}, u32[]{:S(2)}) async-start(bf16[32,96,128]{2,1,0:T(8,128)(2,1)} %param.10), calls=%async_computation.1 | async-start | bytes 1572864 | tf_op jit(solution)/shard_map/all_to_all | solution.py:49
  56.8 3.9 %collective-permute-start.1 = (bf16[4,96,512]{2,1,0:T(8,128)(2,1)S(1)}, bf16[4,96,512]{2,1,0:T(8,128)(2,1)}, u32[]{:S(2)}, u32[]{:S(2)}) collective-permute-start(bf16[4,96,512]{2,1,0:T(8,128)(2,1)S(1)} %slice.113), channel_id=1, source_target_pairs={{0,8},{8,16},{16,24},{1,9},{9,17},{17,25},{2,10},{10,18},{18,26},{... | collective-permute-start | bytes 1179656 | tf_op jit(solution)/shard_map/ppermute | solution.py:14
  60.6 15.5 %all-gather = s32[8,1,128]{2,1,0:T(1,128)S(1)} all-gather(s32[1,1,128]{2,1,0:T(1,128)S(1)} %bitcast.156), channel_id=1, replica_groups=mesh['ctx'=4,'head'=8] {'head'}, dimensions={0}, use_global_device_ids=true | all-gather | bytes 4608 | tf_op jit(solution)/shard_map/all_gather | solution.py:53
  79.0 3.9 %collective-permute-start = (bf16[4,96,512]{2,1,0:T(8,128)(2,1)}, bf16[4,96,512]{2,1,0:T(8,128)(2,1)}, u32[]{:S(2)}, u32[]{:S(2)}) collective-permute-start(bf16[4,96,512]{2,1,0:T(8,128)(2,1)} %slice.110), channel_id=1, source_target_pairs={{0,8},{8,16},{16,24},{1,9},{9,17},{17,25},{2,10},{10,18},{18,26},{... | collective-permute-start | bytes 1179656 | tf_op jit(solution)/shard_map/ppermute | solution.py:14
  90.7 2.1 pad_maximum_fusion
  92.8 2.6 %reshape.175 = bf16[4,96,3,512]{3,2,1,0:T(4,128)(2,1)S(1)} reshape(bf16[4,96,1536]{2,1,0:T(8,128)(2,1)} %pad_maximum_fusion) | data formatting | bytes 2359296 | tf_op jit(solution)/shard_map/reshape | solution.py:63
  98.3 50.2 %while.19 = (s32[]{:T(128)}, bf16[2,4,96,512]{3,2,1,0:T(8,128)(2,1)}, f32[2,4,96,1024]{3,2,1,0:T(8,128)}, f32[2,4,96,1024]{3,2,1,0:T(8,128)}, bf16[2,4,96,1024]{...) while((s32[]{:T(128)}, ...), condition=%wide.region_4.5_spmd.clone, body=%wide.region_0.4_spmd.clone.sunk | while | flops 2439643648 | bytes 138737040 | solution.py:88
  101.1 7.4 %fusion.97 = (f32[4,512]{1,0:T(4,128)S(1)}, f32[4,512,1024]{2,1,0:T(8,128)}) fusion(pred[512,1024]{1,0:T(8,128)(4,1)} %compare_and_fusion.2, bf16[2,4,96,1024]{3,2,1,0:T(8,128)(2,1)S(1)} %get-tuple-element.367, s32[]{:T(128)} %get-tuple-element.350, bf16[2,4,96,512]{3,2,1,0:T(8,128)(2,1)} %get-tuple-element.371), kind=kOutput, calls=%fused_computation.68.clone.1 | convolution fusion | flops 411042816 | bytes 10101760 | tf_op jit(solution)/shard_map/while/body/eval_jaxpr/sub | solution.py:25
  108.5 4.2 %fusion.98 = bf16[4,512,1024]{2,1,0:T(8,128)(2,1)S(1)} fusion(f32[4,512,1024]{2,1,0:T(8,128)} %get-tuple-element.333, f32[4,512]{1,0:T(4,128)S(1)} %get-tuple-element.334), kind=kLoop, calls=%fused_computation.11.clone.1 | loop fusion | flops 4194304 | bytes 12591104 | tf_op jit(solution)/shard_map/while/body/eval_jaxpr/convert_element_type | solution.py:27
  114.9 1.7 copy-done.5
  116.7 1.9 multiply_convert_fusion.3
  119.6 1.7 copy-done.2
  121.3 2.2 fusion.99
  126.1 7.4 %fusion.97 = (f32[4,512]{1,0:T(4,128)S(1)}, f32[4,512,1024]{2,1,0:T(8,128)}) fusion(pred[512,1024]{1,0:T(8,128)(4,1)} %compare_and_fusion.2, bf16[2,4,96,1024]{3,2,1,0:T(8,128)(2,1)S(1)} %get-tuple-element.367, s32[]{:T(128)} %get-tuple-element.350, bf16[2,4,96,512]{3,2,1,0:T(8,128)(2,1)} %get-tuple-element.371), kind=kOutput, calls=%fused_computation.68.clone.1 | convolution fusion | flops 411042816 | bytes 10101760 | tf_op jit(solution)/shard_map/while/body/eval_jaxpr/sub | solution.py:25
  133.4 4.2 %fusion.98 = bf16[4,512,1024]{2,1,0:T(8,128)(2,1)S(1)} fusion(f32[4,512,1024]{2,1,0:T(8,128)} %get-tuple-element.333, f32[4,512]{1,0:T(4,128)S(1)} %get-tuple-element.334), kind=kLoop, calls=%fused_computation.11.clone.1 | loop fusion | flops 4194304 | bytes 12591104 | tf_op jit(solution)/shard_map/while/body/eval_jaxpr/convert_element_type | solution.py:27
  139.9 1.7 copy-done.5
  141.7 1.9 multiply_convert_fusion.3
  144.6 1.7 copy-done.2
  146.3 2.2 fusion.99
  148.5 2.4 copy.46
  150.9 7.2 %all-to-all-start.3 = ((bf16[4,96,1024]{1,0,2:T(4,128)(2,1)}), bf16[4,96,1024]{1,0,2:T(4,128)(2,1)S(1)}, u32[]{:S(2)}, u32[]{:S(2)}) async-start(bf16[4,96,1024]{1,0,2:T(4,128)(2,1)} %bitcast.11), calls=%async_computation.3 | async-start | bytes 2097152 | tf_op jit(solution)/shard_map/all_to_all | solution.py:112
  158.0 1.6 slice_bitcast_fusion
  159.7 1.6 collective-permute-start.3
  162.9 19.1 %collective-permute-done.3 = f32[4,96,512]{2,1,0:T(8,128)S(1)} collective-permute-done((f32[4,96,512]{2,1,0:T(8,128)S(1)}, f32[4,96,512]{2,1,0:T(8,128)S(1)}, u32[]{:S(2)}, u32[]{:S(2)}) %collective-permute-start.3) | collective-permute-done | bytes 786464 | tf_op jit(solution)/shard_map/ppermute | solution.py:14
  183.7 5.3 %all-to-all-start.5 = ((bf16[4,96,1024]{1,0,2:T(4,128)(2,1)}), bf16[4,96,1024]{1,0,2:T(4,128)(2,1)}, u32[]{:S(2)}, u32[]{:S(2)}) async-start(bf16[4,96,1024]{1,0,2:T(4,128)(2,1)} %bitcast.143), calls=%async_computation.5 | async-start | bytes 2097152 | tf_op jit(solution)/shard_map/all_to_all | solution.py:114
  190.3 21.1 %collective-permute-done.2 = f32[4,96,512]{2,1,0:T(8,128)S(1)} collective-permute-done((f32[4,96,512]{2,1,0:T(8,128)}, f32[4,96,512]{2,1,0:T(8,128)S(1)}, u32[]{:S(2)}, u32[]{:S(2)}) %collective-permute-start.2) | collective-permute-done | bytes 786464 | tf_op jit(solution)/shard_map/ppermute | solution.py:14
  213.3 1.6 all-to-all-done.5
  214.9 4.3 %all-to-all-start.4 = ((bf16[4,96,1024]{1,0,2:T(4,128)(2,1)}), bf16[4,96,1024]{1,0,2:T(4,128)(2,1)S(1)}, u32[]{:S(2)}, u32[]{:S(2)}) async-start(bf16[4,96,1024]{1,0,2:T(4,128)(2,1)} %bitcast.19), calls=%async_computation.4 | async-start | bytes 2097152 | tf_op jit(solution)/shard_map/all_to_all | solution.py:113
  220.5 2.2 copy.54
  222.7 22.3 %all-to-all-done.4 = bf16[4,96,1024]{1,0,2:T(4,128)(2,1)S(1)} async-done(((bf16[4,96,1024]{1,0,2:T(4,128)(2,1)}), bf16[4,96,1024]{1,0,2:T(4,128)(2,1)S(1)}, u32[]{:S(2)}, u32[]{:S(2)}) %all-to-all-start.4) | async-done | bytes 786464 | tf_op jit(solution)/shard_map/all_to_all | solution.py:113
  (87 shorter events, 33.8 us)
Async XLA Ops:
  51.4 31.5 %all-to-all-start.1 = ((bf16[32,96,128]{2,1,0:T(8,128)(2,1)}), bf16[32,96,128]{2,1,0:T(8,128)(2,1)S(1)}, u32[]{:S(2)}, u32[]{:S(2)}) async-start(bf16[32,96,128]{2,1,0:T(8,128)(2,1)} %param.10), calls=%async_computation.1 | async-start | bytes 1572864 | tf_op jit(solution)/shard_map/all_to_all | solution.py:49
  55.9 4.8 %copy-start.7 = (s32[128]{0:T(128)S(1)}, s32[128]{0:T(128)}, u32[]{:S(2)}) copy-start(s32[128]{0:T(128)} %param.13) | copy-start | bytes 1540
  56.8 27.9 %collective-permute-start.1 = (bf16[4,96,512]{2,1,0:T(8,128)(2,1)S(1)}, bf16[4,96,512]{2,1,0:T(8,128)(2,1)}, u32[]{:S(2)}, u32[]{:S(2)}) collective-permute-start(bf16[4,96,512]{2,1,0:T(8,128)(2,1)S(1)} %slice.113), channel_id=1, source_target_pairs={{0,8},{8,16},{16,24},{1,9},{9,17},{17,25},{2,10},{10,18},{18,26},{... | collective-permute-start | bytes 1179656 | tf_op jit(solution)/shard_map/ppermute | solution.py:14
  79.0 11.7 %collective-permute-start = (bf16[4,96,512]{2,1,0:T(8,128)(2,1)}, bf16[4,96,512]{2,1,0:T(8,128)(2,1)}, u32[]{:S(2)}, u32[]{:S(2)}) collective-permute-start(bf16[4,96,512]{2,1,0:T(8,128)(2,1)} %slice.110), channel_id=1, source_target_pairs={{0,8},{8,16},{16,24},{1,9},{9,17},{17,25},{2,10},{10,18},{18,26},{... | collective-permute-start | bytes 1179656 | tf_op jit(solution)/shard_map/ppermute | solution.py:14
  108.5 5.6 %copy-start.4 = (f32[2,4,96,1024]{3,2,1,0:T(8,128)S(1)}, f32[2,4,96,1024]{3,2,1,0:T(8,128)}, u32[]{:S(2)}) copy-start(f32[2,4,96,1024]{3,2,1,0:T(8,128)} %get-tuple-element.353) | copy-start | bytes 9437188 | tf_op jit(solution)/shard_map/while
  108.5 8.2 %slice-start = ((s8[8388608]{0:T(1024)(128)(4,1)}), s8[4194304]{0:T(1024)(128)(4,1)S(1)}, s32[]{:S(2)}) async-start(s8[8388608]{0:T(1024)(128)(4,1)} %bitcast.140), calls=%async_computation.6 | async-start | bytes 8388608 | tf_op jit(solution)/shard_map/while
  112.6 4.1 %slice-start.1 = ((s8[8388608]{0:T(1024)(128)(4,1)}), s8[4194304]{0:T(1024)(128)(4,1)S(1)}, s32[]{:S(2)}) async-start(s8[8388608]{0:T(1024)(128)(4,1)} %bitcast.140), calls=%async_computation.7 | async-start | bytes 8388608 | tf_op jit(solution)/shard_map/while
  114.9 1.8 copy-start.5
  116.7 1.9 copy-start
  116.7 2.1 copy-start.1
  119.6 1.7 copy-start.2
  133.4 5.6 %copy-start.4 = (f32[2,4,96,1024]{3,2,1,0:T(8,128)S(1)}, f32[2,4,96,1024]{3,2,1,0:T(8,128)}, u32[]{:S(2)}) copy-start(f32[2,4,96,1024]{3,2,1,0:T(8,128)} %get-tuple-element.353) | copy-start | bytes 9437188 | tf_op jit(solution)/shard_map/while
  133.4 8.2 %slice-start = ((s8[8388608]{0:T(1024)(128)(4,1)}), s8[4194304]{0:T(1024)(128)(4,1)S(1)}, s32[]{:S(2)}) async-start(s8[8388608]{0:T(1024)(128)(4,1)} %bitcast.140), calls=%async_computation.6 | async-start | bytes 8388608 | tf_op jit(solution)/shard_map/while
  137.6 4.1 %slice-start.1 = ((s8[8388608]{0:T(1024)(128)(4,1)}), s8[4194304]{0:T(1024)(128)(4,1)S(1)}, s32[]{:S(2)}) async-start(s8[8388608]{0:T(1024)(128)(4,1)} %bitcast.140), calls=%async_computation.7 | async-start | bytes 8388608 | tf_op jit(solution)/shard_map/while
  139.9 1.8 copy-start.5
  141.7 1.9 copy-start
  141.7 2.1 copy-start.1
  144.6 1.7 copy-start.2
  150.9 32.9 %all-to-all-start.3 = ((bf16[4,96,1024]{1,0,2:T(4,128)(2,1)}), bf16[4,96,1024]{1,0,2:T(4,128)(2,1)S(1)}, u32[]{:S(2)}, u32[]{:S(2)}) async-start(bf16[4,96,1024]{1,0,2:T(4,128)(2,1)} %bitcast.11), calls=%async_computation.3 | async-start | bytes 2097152 | tf_op jit(solution)/shard_map/all_to_all | solution.py:112
  158.0 3.2 %copy-start.3 = (f32[2,4,96,1024]{3,2,1,0:T(8,128)S(1)}, f32[2,4,96,1024]{3,2,1,0:T(8,128)}, u32[]{:S(2)}) copy-start(f32[2,4,96,1024]{3,2,1,0:T(8,128)} %get-tuple-element.179) | copy-start | bytes 9437188
  159.7 2.6 %copy-start.6 = (f32[2,4,96,1024]{3,2,1,0:T(8,128)S(1)}, f32[2,4,96,1024]{3,2,1,0:T(8,128)}, u32[]{:S(2)}) copy-start(f32[2,4,96,1024]{3,2,1,0:T(8,128)} %get-tuple-element.180) | copy-start | bytes 9437188
  159.7 22.3 %collective-permute-start.3 = (f32[4,96,512]{2,1,0:T(8,128)S(1)}, f32[4,96,512]{2,1,0:T(8,128)S(1)}, u32[]{:S(2)}, u32[]{:S(2)}) collective-permute-start(f32[4,96,512]{2,1,0:T(8,128)S(1)} %get-tuple-element.258), channel_id=1, source_target_pairs={{8,0},{16,8},{24,16},{9,1},{17,9},{25,17},{10,2},{18,10},{26,18},{... | collective-permute-start | bytes 2359304 | tf_op jit(solution)/shard_map/ppermute | solution.py:14
  183.7 31.1 %all-to-all-start.5 = ((bf16[4,96,1024]{1,0,2:T(4,128)(2,1)}), bf16[4,96,1024]{1,0,2:T(4,128)(2,1)}, u32[]{:S(2)}, u32[]{:S(2)}) async-start(bf16[4,96,1024]{1,0,2:T(4,128)(2,1)} %bitcast.143), calls=%async_computation.5 | async-start | bytes 2097152 | tf_op jit(solution)/shard_map/all_to_all | solution.py:114
  189.1 22.4 %collective-permute-start.2 = (f32[4,96,512]{2,1,0:T(8,128)}, f32[4,96,512]{2,1,0:T(8,128)S(1)}, u32[]{:S(2)}, u32[]{:S(2)}) collective-permute-start(f32[4,96,512]{2,1,0:T(8,128)} %get-tuple-element.260), channel_id=1, source_target_pairs={{8,0},{16,8},{24,16},{9,1},{17,9},{25,17},{10,2},{18,10},{26,18},{... | collective-permute-start | bytes 2359304 | tf_op jit(solution)/shard_map/ppermute | solution.py:14
  214.9 30.1 %all-to-all-start.4 = ((bf16[4,96,1024]{1,0,2:T(4,128)(2,1)}), bf16[4,96,1024]{1,0,2:T(4,128)(2,1)S(1)}, u32[]{:S(2)}, u32[]{:S(2)}) async-start(bf16[4,96,1024]{1,0,2:T(4,128)(2,1)} %bitcast.19), calls=%async_computation.4 | async-start | bytes 2097152 | tf_op jit(solution)/shard_map/all_to_all | solution.py:113
where the time goes:
time: 248 us; the launch traced here: 246 us
  blocking collectives  66.3 us (27%)
  waiting for transfers between devices  65.3 us (26%)
  local copies, waits for them, and re-layouts  32.5 us (13%)
  starting transfers between devices  31.9 us (13%)
  matrix products  29 us (12%)
  other arithmetic  18.7 us (8%)
    ppermute x4, waiting for transfers between devices, from_behind(): lax.ppermute(value, axis, [(source, source + steps) for source in range(f...  41.4 us
    all_to_all x1, blocking collectives, shards(): lax.all_to_all(values, 'head', split_axis=0, concat_axis=2, tiled=True)  26.3 us
    all_to_all x1, blocking collectives, shards(): lax.all_to_all(keys, 'head', split_axis=0, concat_axis=2, tiled=True)  24.4 us
    all_to_all x1, waiting for transfers between devices, shards(): lax.all_to_all(grad_k, 'head', split_axis=2, concat_axis=0, tiled=True)  22.3 us
    all_gather x1, blocking collectives, shards(): starts = lax.all_gather(doc_start, 'head', axis=0, tiled=True)  15.5 us
    sub x2, matrix products, block_grads(): weights = jnp.exp(scores - row_peak)  14.7 us
    ppermute x4, starting transfers between devices, from_behind(): lax.ppermute(value, axis, [(source, source + steps) for source in range(f...  10.6 us
    convert_element_type x2, other arithmetic, block_grads(): probs_low = soft_probs.astype(jnp.bfloat16)  8.31 us
  transfers between devices with their start and end apart: 8, of which 5 were waited for; matrix products, arithmetic and copies ran while one was open for 8% of the time, Pallas kernels for 0%

commit v1 on v0

--- a/solution.py
+++ b/solution.py
@@ -1,11 +1,16 @@
+import functools
 import math
 
 import jax
 import jax.numpy as jnp
 from jax import lax
+from jax.experimental import pallas as pl
+from jax.experimental.pallas import tpu as pltpu
 from jax.sharding import PartitionSpec as P
 
 DOC_MAX = 512
+PIECE = 2
+MESH = pl.DeviceIdType.MESH
 
 
 def from_behind(value, axis, steps):
@@ -115,20 +120,272 @@
     )
 
 
+def chunk_kernel(
+    n_ctx, n_head, q_ref, k_ref, v_ref, doc_ref, dq_ref, dk_ref, dv_ref,
+    qbuf, kvbuf, dbuf, bias, stage_q, stage_kv, part,
+    in_s, in_r, loc_in, doc_s, doc_r, l_s, l_r, g_s, g_r, o_s, o_r, loc_out,
+):
+    heads, depth, toks = q_ref.shape
+    half = heads // 2
+    pieces = half // PIECE
+    scale = 1.0 / math.sqrt(depth)
+    me = lax.axis_index("ctx") * n_head + lax.axis_index("head")
+    chip, core = me // 2, me % 2
+    mate = 1 - core
+    last = n_ctx * n_head // 2 - 1
+    odd = chip % 2
+    is_left = (chip == 0) | ((odd == 1) & (chip >= 3) & (chip < last))
+    is_right = (chip == 1) | ((odd == 0) & (chip >= 4))
+    paired = is_left | is_right
+    other_chip = jnp.where(is_left, chip + 1, chip - 1)
+
+    def device(chip_id, core_id):
+        linear = chip_id * 2 + core_id
+        return (linear // n_head, linear % n_head)
+
+    mate_id = device(chip, mate)
+
+    def remote(src, dst, send, recv, to):
+        return pltpu.make_async_remote_copy(
+            src_ref=src, dst_ref=dst, send_sem=send, recv_sem=recv, device_id=to, device_id_type=MESH
+        )
+
+    def span(base, p):
+        return pl.ds(base + p * PIECE, PIECE)
+
+    def mate_in(i, p):
+        src = (q_ref, k_ref, v_ref)[i].at[span(mate * half, p)]
+        dst = qbuf.at[core, span(0, p)] if i == 0 else kvbuf.at[i - 1, 2 + core, span(0, p)]
+        return remote(src, dst, in_s.at[i, p], in_r.at[i, p], mate_id)
+
+    def own_in(i):
+        src = (q_ref, k_ref, v_ref)[i].at[pl.ds(core * half, half)]
+        dst = qbuf.at[core] if i == 0 else kvbuf.at[i - 1, 2 + core]
+        return pltpu.make_async_copy(src, dst, loc_in.at[i])
+
+    def doc_copy():
+        return remote(doc_ref, dbuf.at[core], doc_s.at[0], doc_r.at[0], mate_id)
+
+    def ahead(i, j, p):
+        src = (k_ref, v_ref)[i].at[span(j * half, p)]
+        return remote(
+            src, kvbuf.at[i, core, span(0, p)], l_s.at[i, j, p], l_r.at[i, core, p], device(other_chip, j)
+        )
+
+    def ahead_arrival(i, j, p):
+        src = (k_ref, v_ref)[i].at[span(j * half, p)]
+        return remote(
+            src, kvbuf.at[i, j, span(0, p)], l_s.at[i, j, p], l_r.at[i, j, p], device(other_chip, j)
+        )
+
+    def back(i, j, p):
+        return remote(
+            stage_kv.at[i, j, span(0, p)], part.at[i, core, span(0, p)],
+            g_s.at[i, j, p], g_r.at[i, core, p], device(other_chip, j),
+        )
+
+    def back_arrival(i, j, p):
+        return remote(
+            stage_kv.at[i, j, span(0, p)], part.at[i, j, span(0, p)],
+            g_s.at[i, j, p], g_r.at[i, j, p], device(other_chip, j),
+        )
+
+    def staged(i, whose, p):
+        return stage_q.at[whose, span(0, p)] if i == 0 else stage_kv.at[i - 1, 2 + whose, span(0, p)]
+
+    def mate_out(i, p):
+        dst = (dq_ref, dk_ref, dv_ref)[i].at[span(core * half, p)]
+        return remote(staged(i, mate, p), dst, o_s.at[i, p], o_r.at[i, p], mate_id)
+
+    def mate_out_arrival(i, p):
+        dst = (dq_ref, dk_ref, dv_ref)[i].at[span(mate * half, p)]
+        return remote(staged(i, mate, p), dst, o_s.at[i, p], o_r.at[i, p], mate_id)
+
+    def own_out(i, p):
+        dst = (dq_ref, dk_ref, dv_ref)[i].at[span(core * half, p)]
+        return pltpu.make_async_copy(staged(i, core, p), dst, loc_out.at[i, p])
+
+    def each(body):
+        lax.fori_loop(0, pieces, lambda p, carry: (body(p), carry)[1], 0)
+
+    barrier = pltpu.get_barrier_semaphore()
+    pl.semaphore_signal(barrier, inc=1, device_id=mate_id, device_id_type=MESH)
+
+    @pl.when(paired)
+    def _():
+        for j in range(2):
+            pl.semaphore_signal(barrier, inc=1, device_id=device(other_chip, j), device_id_type=MESH)
+        pl.semaphore_wait(barrier, 3)
+
+    @pl.when(jnp.logical_not(paired))
+    def _():
+        pl.semaphore_wait(barrier, 1)
+
+    @pl.when(is_left)
+    def _():
+        def send(p):
+            for j in range(2):
+                for i in range(2):
+                    ahead(i, j, p).start()
+
+        each(send)
+
+    doc_copy().start()
+    for i in range(3):
+        own_in(i).start()
+
+    def send_mate(p):
+        for i in range(3):
+            mate_in(i, p).start()
+
+    each(send_mate)
+    dbuf[core] = doc_ref[...]
+    for i in range(3):
+        own_in(i).wait()
+    doc_copy().wait_send()
+    remote(doc_ref, dbuf.at[mate], doc_s.at[0], doc_r.at[0], mate_id).wait_recv()
+
+    wide = 2 * toks
+    base = chip * wide
+    first = jnp.concatenate([dbuf[0], dbuf[1]], axis=1)
+    query_pos = base + lax.broadcasted_iota(jnp.int32, (2 * wide, wide), 1)
+    key_pos = base - wide + lax.broadcasted_iota(jnp.int32, (2 * wide, wide), 0)
+    bias[...] = jnp.where((key_pos >= first) & (key_pos <= query_pos), 0.0, -jnp.inf)
+
+    def one_head(h, slots):
+        query = jnp.concatenate([qbuf[0, h], qbuf[1, h]], axis=1)
+        key = jnp.concatenate([kvbuf[0, s, h] for s in slots], axis=1)
+        value = jnp.concatenate([kvbuf[1, s, h] for s in slots], axis=1)
+        rows = pl.ds(slots[0] * toks, len(slots) * toks)
+        dot = functools.partial(lax.dot_general, preferred_element_type=jnp.float32)
+        tn, nn, nt = ((((0,), (0,)), ((), ())), (((1,), (0,)), ((), ())), (((1,), (1,)), ((), ())))
+        scores = dot(key, query, tn) * (scale * math.log2(math.e)) + bias[rows, :]
+        weights = jnp.exp2(scores - jnp.max(scores, axis=0, keepdims=True))
+        probs = weights * (1.0 / jnp.sum(weights, axis=0, keepdims=True))
+        low = probs.astype(jnp.bfloat16)
+        attended = dot(value, low, nn).astype(jnp.bfloat16)
+        wide_att = attended.astype(jnp.float32)
+        row_dot = jnp.sum(wide_att * wide_att, axis=0, keepdims=True)
+        grad_probs = dot(value, attended, tn)
+        grad_scores = (probs * (grad_probs - row_dot)).astype(jnp.bfloat16)
+        grad_q = (dot(key, grad_scores, nn) * scale).astype(jnp.bfloat16)
+        grad_k = (dot(query, grad_scores, nt) * scale).astype(jnp.bfloat16)
+        grad_v = dot(attended, low, nt).astype(jnp.bfloat16)
+        for j in range(2):
+            stage_q[j, h] = grad_q[:, j * toks : (j + 1) * toks]
+        for n, s in enumerate(slots):
+            stage_kv[0, s, h] = grad_k[:, n * toks : (n + 1) * toks]
+            stage_kv[1, s, h] = grad_v[:, n * toks : (n + 1) * toks]
+
+    def work(p, slots):
+        for i in range(3):
+            dst = qbuf.at[mate, span(0, p)] if i == 0 else kvbuf.at[i - 1, 2 + mate, span(0, p)]
+            src = (q_ref, k_ref, v_ref)[i].at[span(mate * half, p)]
+            remote(src, dst, in_s.at[i, p], in_r.at[i, p], mate_id).wait_recv()
+        for n in range(PIECE):
+            one_head(p * PIECE + n, slots)
+        for i in range(3):
+            mate_out(i, p).start()
+            own_out(i, p).start()
+
+    @pl.when(is_right)
+    def _():
+        def step(p):
+            for j in range(2):
+                for i in range(2):
+                    ahead_arrival(i, j, p).wait_recv()
+            work(p, (0, 1, 2, 3))
+            for j in range(2):
+                for i in range(2):
+                    back(i, j, p).start()
+
+        each(step)
+
+    @pl.when(jnp.logical_not(is_right))
+    def _():
+        each(lambda p: work(p, (2, 3)))
+
+    def drain(p):
+        for i in range(3):
+            mate_in(i, p).wait_send()
+            own_out(i, p).wait()
+            mate_out(i, p).wait_send()
+            mate_out_arrival(i, p).wait_recv()
+
+    each(drain)
+
+    @pl.when(is_left)
+    def _():
+        def add(p):
+            for i in range(2):
+                out = (dk_ref, dv_ref)[i]
+                for j in range(2):
+                    ahead(i, j, p).wait_send()
+                    back_arrival(i, j, p).wait_recv()
+                    at = span(j * half, p)
+                    total = out[at].astype(jnp.float32) + part[i, j, span(0, p)].astype(jnp.float32)
+                    out[at] = total.astype(jnp.bfloat16)
+
+        each(add)
+
+    @pl.when(is_right)
+    def _():
+        def sent(p):
+            for j in range(2):
+                for i in range(2):
+                    back(i, j, p).wait_send()
+
+        each(sent)
+
+
+def chunk_shards(n_ctx, n_head, queries, keys, values, doc_start):
+    heads, depth, toks = queries.shape
+    half = heads // 2
+    pieces = half // PIECE
+    like = jax.ShapeDtypeStruct(queries.shape, jnp.bfloat16)
+    vmem = pl.BlockSpec(memory_space=pltpu.VMEM)
+    low, sem = jnp.bfloat16, pltpu.SemaphoreType.DMA
+    return pl.pallas_call(
+        functools.partial(chunk_kernel, n_ctx, n_head),
+        out_shape=(like, like, like),
+        in_specs=[vmem] * 4,
+        out_specs=(vmem,) * 3,
+        scratch_shapes=[
+            pltpu.VMEM((2, half, depth, toks), low),
+            pltpu.VMEM((2, 4, half, depth, toks), low),
+            pltpu.VMEM((2, 1, toks), jnp.int32),
+            pltpu.VMEM((4 * toks, 2 * toks), jnp.float32),
+            pltpu.VMEM((2, half, depth, toks), low),
+            pltpu.VMEM((2, 4, half, depth, toks), low),
+            pltpu.VMEM((2, 2, half, depth, toks), low),
+            sem((3, pieces)), sem((3, pieces)), sem((3,)), sem((1,)), sem((1,)),
+            sem((2, 2, pieces)), sem((2, 2, pieces)), sem((2, 2, pieces)), sem((2, 2, pieces)),
+            sem((3, pieces)), sem((3, pieces)), sem((3, pieces)),
+        ],
+        compiler_params=pltpu.CompilerParams(
+            collective_id=0, has_side_effects=True, vmem_limit_bytes=40 * 1024 * 1024
+        ),
+        cost_estimate=pl.CostEstimate(
+            flops=12 * half * 8 * toks * toks * depth, bytes_accessed=12 * heads * depth * toks,
+            transcendentals=8 * half * toks * toks,
+        ),
+    )(queries, keys, values, doc_start.reshape(1, toks))
+
+
 def solution(mesh):
+    n_ctx, n_head = mesh.shape["ctx"], mesh.shape["head"]
+
+    def program(queries, keys, values, doc_start):
+        toks = queries.shape[2]
+        if 4 * toks == DOC_MAX and n_head * toks == 2 * DOC_MAX and queries.shape[0] % (2 * PIECE) == 0:
+            return chunk_shards(n_ctx, n_head, queries, keys, values, doc_start)
+        return shards(queries, keys, values, doc_start)
+
+    spec = P(None, None, ("ctx", "head"))
     return jax.shard_map(
-        shards,
+        program,
         mesh=mesh,
-        in_specs=(
-            P(None, None, ("ctx", "head")),
-            P(None, None, ("ctx", "head")),
-            P(None, None, ("ctx", "head")),
-            P(("ctx", "head")),
-        ),
-        out_specs=(
-            P(None, None, ("ctx", "head")),
-            P(None, None, ("ctx", "head")),
-            P(None, None, ("ctx", "head")),
-        ),
+        in_specs=(spec, spec, spec, P(("ctx", "head"))),
+        out_specs=(spec, spec, spec),
         check_vma=False,
     )

time: 248 us -> 88.3 us (0.36)
  the two profiles are of different devices: /device:TPU:1 before, /device:TPU:13 now
where the time goes in v1:
time: 88.3 us; the launch traced here: 88 us
  Pallas kernels  80.7 us (91%)
  local copies, waits for them, and re-layouts  6.69 us (8%)
    pallas_call x1, Pallas kernels, chunk_shards(): pl.pallas_call(functools.partial(chunk_kernel, n_ctx, n_head), out_shape=...  80.7 us
    unnamed x11, local copies, waits for them, and re-layouts  6.69 us

profile of v1, /device:TPU:13, one launch (start us, length us, event | category | flops | bytes accessed | tf_op | source)
XLA Modules:
  0.0 88.0 jit_solution(17418209791343934922)
XLA Ops:
  0.6 0.0 copy-start.3
  0.6 0.6 copy-done.3
  1.3 0.0 copy-start
  1.3 1.1 %copy-done = bf16[32,96,128]{2,1,0:T(8,128)(2,1)S(1)} copy-done((bf16[32,96,128]{2,1,0:T(8,128)(2,1)S(1)}, bf16[32,96,128]{2,1,0:T(8,128)(2,1)}, u32[]{:S(2)}) %copy-start) | copy-done | bytes 786456
  2.4 0.0 copy-start.1
  2.4 1.1 %copy-done.1 = bf16[32,96,128]{2,1,0:T(8,128)(2,1)S(1)} copy-done((bf16[32,96,128]{2,1,0:T(8,128)(2,1)S(1)}, bf16[32,96,128]{2,1,0:T(8,128)(2,1)}, u32[]{:S(2)}) %copy-start.1) | copy-done | bytes 786456
  3.6 0.0 copy-start.2
  3.6 1.1 %copy-done.2 = bf16[32,96,128]{2,1,0:T(8,128)(2,1)S(1)} copy-done((bf16[32,96,128]{2,1,0:T(8,128)(2,1)S(1)}, bf16[32,96,128]{2,1,0:T(8,128)(2,1)}, u32[]{:S(2)}) %copy-start.2) | copy-done | bytes 786456
  4.7 80.7 %shard_map.67 = (bf16[32,96,128]{2,1,0:T(8,128)(2,1)S(1)}, bf16[32,96,128]{2,1,0:T(8,128)(2,1)S(1)}, bf16[32,96,128]{2,1,0:T(8,128)(2,1)S(1)}) custom-call(bf16[32,96,128]{2,1,0:T(8,128)(2,1)S(1)} %copy-done, bf16[32,96,128]{2,1,0:T(8,128)(2,1)S(1)} %copy-done.1, bf16[32,96,128]{2,1,0:T(8,128)(2,1)S(1)} %copy-done.2, s32[1,128]{1,0:T(1,128)S(1)} %bitcast.1), custom_call_target="tpu_custom_call" | custom-call | flops 2415919104 | bytes 4718592 | tf_op jit(solution)/shard_map/pallas_call | solution.py:348
  85.4 0.9 %copy.10 = bf16[32,96,128]{2,1,0:T(8,128)(2,1)} copy(bf16[32,96,128]{2,1,0:T(8,128)(2,1)S(1)} %get-tuple-element.6) | data formatting | bytes 1572864
  86.3 0.9 copy.11
  87.2 0.9 copy.12
Async XLA Ops:
  0.6 0.7 copy-start.3
  1.3 1.1 %copy-start = (bf16[32,96,128]{2,1,0:T(8,128)(2,1)S(1)}, bf16[32,96,128]{2,1,0:T(8,128)(2,1)}, u32[]{:S(2)}) copy-start(bf16[32,96,128]{2,1,0:T(8,128)(2,1)} %q_ref.1) | copy-start | bytes 2359300
  2.4 1.1 %copy-start.1 = (bf16[32,96,128]{2,1,0:T(8,128)(2,1)S(1)}, bf16[32,96,128]{2,1,0:T(8,128)(2,1)}, u32[]{:S(2)}) copy-start(bf16[32,96,128]{2,1,0:T(8,128)(2,1)} %k_ref.1) | copy-start | bytes 2359300
  3.6 1.1 %copy-start.2 = (bf16[32,96,128]{2,1,0:T(8,128)(2,1)S(1)}, bf16[32,96,128]{2,1,0:T(8,128)(2,1)}, u32[]{:S(2)}) copy-start(bf16[32,96,128]{2,1,0:T(8,128)(2,1)} %v_ref.1) | copy-start | bytes 2359300

commit v2 on v1

--- a/solution.py
+++ b/solution.py
@@ -290,16 +290,24 @@
 
     @pl.when(is_right)
     def _():
+        def send_back(p):
+            for j in range(2):
+                for i in range(2):
+                    back(i, j, p).start()
+
         def step(p):
             for j in range(2):
                 for i in range(2):
                     ahead_arrival(i, j, p).wait_recv()
+
+            @pl.when(p == pieces - 1)
+            def _():
+                lax.fori_loop(0, pieces - 1, lambda e, carry: (send_back(e), carry)[1], 0)
+
             work(p, (0, 1, 2, 3))
-            for j in range(2):
-                for i in range(2):
-                    back(i, j, p).start()
 
         each(step)
+        send_back(pieces - 1)
 
     @pl.when(jnp.logical_not(is_right))
     def _():
@@ -348,7 +356,7 @@
     return pl.pallas_call(
         functools.partial(chunk_kernel, n_ctx, n_head),
         out_shape=(like, like, like),
-        in_specs=[vmem] * 4,
+        in_specs=[pl.BlockSpec(memory_space=pltpu.HBM)] * 3 + [vmem],
         out_specs=(vmem,) * 3,
         scratch_shapes=[
             pltpu.VMEM((2, half, depth, toks), low),
@@ -363,7 +371,7 @@
             sem((3, pieces)), sem((3, pieces)), sem((3, pieces)),
         ],
         compiler_params=pltpu.CompilerParams(
-            collective_id=0, has_side_effects=True, vmem_limit_bytes=40 * 1024 * 1024
+            collective_id=0, has_side_effects=True, vmem_limit_bytes=60 * 1024 * 1024
         ),
         cost_estimate=pl.CostEstimate(
             flops=12 * half * 8 * toks * toks * depth, bytes_accessed=12 * heads * depth * toks,

time: 88.3 us -> 84.9 us (0.961)
  the two profiles are of different devices: /device:TPU:13 before, /device:TPU:1 now
where the time goes in v2:
time: 84.9 us; the launch traced here: 83.6 us
  Pallas kernels  78.5 us (92%)
  local copies, waits for them, and re-layouts  4.44 us (5%)
    pallas_call x1, Pallas kernels, chunk_shards(): pl.pallas_call(functools.partial(chunk_kernel, n_ctx, n_head), out_shape=...  78.5 us
    unnamed x7, local copies, waits for them, and re-layouts  4.44 us

profile of v2, /device:TPU:1, one launch (start us, length us, event | category | flops | bytes accessed | tf_op | source)
XLA Modules:
  0.0 83.6 jit_solution(9607118581576463910)
XLA Ops:
  0.6 78.5 %shard_map.67 = (bf16[32,96,128]{2,1,0:T(8,128)(2,1)}, bf16[32,96,128]{2,1,0:T(8,128)(2,1)}, bf16[32,96,128]{2,1,0:T(8,128)(2,1)}) custom-call(bf16[32,96,128]{2,1,0:T(8,128)(2,1)} %q_ref.1, bf16[32,96,128]{2,1,0:T(8,128)(2,1)} %k_ref.1, bf16[32,96,128]{2,1,0:T(8,128)(2,1)} %v_ref.1, s32[1,128]{1,0:T(1,128)} %bitcast.1), custom_call_target="tpu_custom_call" | custom-call | flops 2415919104 | bytes 4718592 | tf_op jit(solution)/shard_map/pallas_call | solution.py:356
  79.2 0.0 copy-start.1
  79.2 2.1 %copy.10 = bf16[32,96,128]{2,1,0:T(8,128)(2,1)} copy(bf16[32,96,128]{2,1,0:T(8,128)(2,1)} %get-tuple-element.6) | data formatting | bytes 1572864
  81.3 0.0 copy-done.1
  81.3 0.0 copy-start
  81.3 0.9 %copy.11 = bf16[32,96,128]{2,1,0:T(8,128)(2,1)} copy(bf16[32,96,128]{2,1,0:T(8,128)(2,1)S(1)} %copy-done.1) | data formatting | bytes 1572864
  82.2 0.5 copy-done
  82.7 0.9 %copy.12 = bf16[32,96,128]{2,1,0:T(8,128)(2,1)} copy(bf16[32,96,128]{2,1,0:T(8,128)(2,1)S(1)} %copy-done) | data formatting | bytes 1572864
Async XLA Ops:
  79.2 2.1 %copy-start.1 = (bf16[32,96,128]{2,1,0:T(8,128)(2,1)S(1)}, bf16[32,96,128]{2,1,0:T(8,128)(2,1)}, u32[]{:S(2)}) copy-start(bf16[32,96,128]{2,1,0:T(8,128)(2,1)} %get-tuple-element.7) | copy-start | bytes 2359300
  81.3 1.4 %copy-start = (bf16[32,96,128]{2,1,0:T(8,128)(2,1)S(1)}, bf16[32,96,128]{2,1,0:T(8,128)(2,1)}, u32[]{:S(2)}) copy-start(bf16[32,96,128]{2,1,0:T(8,128)(2,1)} %get-tuple-element.8) | copy-start | bytes 2359300

commit v3 on v2

--- a/solution.py
+++ b/solution.py
@@ -10,6 +10,7 @@
 
 DOC_MAX = 512
 PIECE = 2
+DETOUR = 2
 MESH = pl.DeviceIdType.MESH
 
 
@@ -123,7 +124,7 @@
 def chunk_kernel(
     n_ctx, n_head, q_ref, k_ref, v_ref, doc_ref, dq_ref, dk_ref, dv_ref,
     qbuf, kvbuf, dbuf, bias, stage_q, stage_kv, part,
-    in_s, in_r, loc_in, doc_s, doc_r, l_s, l_r, g_s, g_r, o_s, o_r, loc_out,
+    in_s, in_r, loc_in, doc_s, doc_r, l_s, l_r, g_s, g_r, o_s, o_r, loc_out, rbuf, r_s, r_r,
 ):
     heads, depth, toks = q_ref.shape
     half = heads // 2
@@ -139,6 +140,21 @@
     paired = is_left | is_right
     other_chip = jnp.where(is_left, chip + 1, chip - 1)
 
+    flows = n_ctx - 1
+    items = flows * DETOUR
+    chained = paired & (chip >= 3)
+    flow = (chip + 1) // 4 - 1
+    far = (chip + 1) % 4 < 2
+    ahead_relay, back_relay = jnp.where(far, last, 1), jnp.where(far, 0, 2)
+    relays_ahead = (chip == last) | (chip == 1)
+    relays_back = (chip == 0) | (chip == 2)
+    relays = relays_ahead | relays_back
+    far_relay = (chip == last) | (chip == 0)
+
+    def relay_ends(f):
+        left = 4 * f + 4 + jnp.where(far_relay, -1, 1)
+        return jnp.where(relays_ahead, left, left + 1), jnp.where(relays_ahead, left + 1, left)
+
     def device(chip_id, core_id):
         linear = chip_id * 2 + core_id
         return (linear // n_head, linear % n_head)
@@ -190,6 +206,45 @@
             g_s.at[i, j, p], g_r.at[i, j, p], device(other_chip, j),
         )
 
+    def ahead_detour(i, j, r):
+        p = pieces - DETOUR + r
+        src = (k_ref, v_ref)[i].at[span(j * half, p)]
+        return remote(
+            src, rbuf.at[flow, i, j, r], l_s.at[i, j, p], r_r.at[flow, i, j, r], device(ahead_relay, core)
+        )
+
+    def back_detour(i, j, r):
+        return remote(
+            stage_kv.at[i, j, span(0, r)], rbuf.at[flow, i, j, r],
+            g_s.at[i, j, r], r_r.at[flow, i, j, r], device(back_relay, core),
+        )
+
+    def detour_arrival(f, i, j, r):
+        return remote(
+            rbuf.at[f, i, j, r], rbuf.at[f, i, j, r], r_s.at[f, i, j, r], r_r.at[f, i, j, r],
+            device(relay_ends(f)[1], j),
+        )
+
+    def ahead_onward(f, i, j, r):
+        p = pieces - DETOUR + r
+        return remote(
+            rbuf.at[f, i, j, r], kvbuf.at[i, core, span(0, p)],
+            r_s.at[f, i, j, r], l_r.at[i, core, p], device(relay_ends(f)[1], j),
+        )
+
+    def back_onward(f, i, j, r):
+        return remote(
+            rbuf.at[f, i, j, r], part.at[i, core, span(0, r)],
+            r_s.at[f, i, j, r], g_r.at[i, core, r], device(relay_ends(f)[1], j),
+        )
+
+    def relay(onward, item):
+        f, r = item % flows, item // flows
+        for j in range(2):
+            for i in range(2):
+                detour_arrival(f, i, j, r).wait_recv()
+                onward(f, i, j, r).start()
+
     def staged(i, whose, p):
         return stage_q.at[whose, span(0, p)] if i == 0 else stage_kv.at[i - 1, 2 + whose, span(0, p)]
 
@@ -215,11 +270,29 @@
     def _():
         for j in range(2):
             pl.semaphore_signal(barrier, inc=1, device_id=device(other_chip, j), device_id_type=MESH)
-        pl.semaphore_wait(barrier, 3)
-
-    @pl.when(jnp.logical_not(paired))
-    def _():
-        pl.semaphore_wait(barrier, 1)
+
+    @pl.when(chained)
+    def _():
+        single = jnp.where(is_left, ahead_relay, back_relay)
+        double = jnp.where(is_left, back_relay, ahead_relay)
+        for to in (device(single, core), device(double, 0), device(double, 1)):
+            pl.semaphore_signal(barrier, inc=1, device_id=to, device_id_type=MESH)
+        pl.semaphore_wait(barrier, 6)
+
+    @pl.when(relays)
+    def _():
+        for f in range(flows):
+            single, double = relay_ends(f)
+            for to in (device(single, core), device(double, 0), device(double, 1)):
+                pl.semaphore_signal(barrier, inc=1, device_id=to, device_id_type=MESH)
+
+    @pl.when(relays & paired)
+    def _():
+        pl.semaphore_wait(barrier, 3 + 3 * flows)
+
+    @pl.when(relays & jnp.logical_not(paired))
+    def _():
+        pl.semaphore_wait(barrier, 1 + 3 * flows)
 
     @pl.when(is_left)
     def _():
@@ -228,7 +301,19 @@
                 for i in range(2):
                     ahead(i, j, p).start()
 
-        each(send)
+        @pl.when(chained)
+        def _():
+            for r in range(DETOUR):
+                for j in range(2):
+                    for i in range(2):
+                        ahead_detour(i, j, r).start()
+
+        lax.fori_loop(0, pieces - DETOUR, lambda p, carry: (send(p), carry)[1], 0)
+
+        @pl.when(jnp.logical_not(chained))
+        def _():
+            for r in range(DETOUR):
+                send(pieces - DETOUR + r)
 
     doc_copy().start()
     for i in range(3):
@@ -295,23 +380,48 @@
                 for i in range(2):
                     back(i, j, p).start()
 
+        def send_most():
+            for r in range(DETOUR):
+                for j in range(2):
+                    for i in range(2):
+                        back_detour(i, j, r).start()
+            lax.fori_loop(DETOUR, pieces - 1, lambda e, carry: (send_back(e), carry)[1], 0)
+
         def step(p):
             for j in range(2):
                 for i in range(2):
                     ahead_arrival(i, j, p).wait_recv()
 
-            @pl.when(p == pieces - 1)
+            @pl.when(chained & (p == pieces - 1))
             def _():
-                lax.fori_loop(0, pieces - 1, lambda e, carry: (send_back(e), carry)[1], 0)
+                send_most()
 
             work(p, (0, 1, 2, 3))
 
+            @pl.when(jnp.logical_not(chained))
+            def _():
+                send_back(p)
+
+                @pl.when(p < items)
+                def _():
+                    relay(ahead_onward, p)
+
         each(step)
-        send_back(pieces - 1)
+
+        @pl.when(chained)
+        def _():
+            send_back(pieces - 1)
 
     @pl.when(jnp.logical_not(is_right))
     def _():
-        each(lambda p: work(p, (2, 3)))
+        def step(p):
+            work(p, (2, 3))
+
+            @pl.when((chip == last) & (p < items))
+            def _():
+                relay(ahead_onward, p)
+
+        each(step)
 
     def drain(p):
         for i in range(3):
@@ -321,6 +431,10 @@
             mate_out_arrival(i, p).wait_recv()
 
     each(drain)
+
+    @pl.when(relays_back)
+    def _():
+        lax.fori_loop(0, items, lambda t, carry: (relay(back_onward, t), carry)[1], 0)
 
     @pl.when(is_left)
     def _():
@@ -344,6 +458,15 @@
                     back(i, j, p).wait_send()
 
         each(sent)
+
+    @pl.when(relays)
+    def _():
+        def onward_sent(t):
+            for j in range(2):
+                for i in range(2):
+                    ahead_onward(t % flows, i, j, t // flows).wait_send()
+
+        lax.fori_loop(0, items, lambda t, carry: (onward_sent(t), carry)[1], 0)
 
 
 def chunk_shards(n_ctx, n_head, queries, keys, values, doc_start):
@@ -369,6 +492,8 @@
             sem((3, pieces)), sem((3, pieces)), sem((3,)), sem((1,)), sem((1,)),
             sem((2, 2, pieces)), sem((2, 2, pieces)), sem((2, 2, pieces)), sem((2, 2, pieces)),
             sem((3, pieces)), sem((3, pieces)), sem((3, pieces)),
+            pltpu.VMEM((n_ctx - 1, 2, 2, DETOUR, PIECE, depth, toks), low),
+            sem((n_ctx - 1, 2, 2, DETOUR)), sem((n_ctx - 1, 2, 2, DETOUR)),
         ],
         compiler_params=pltpu.CompilerParams(
             collective_id=0, has_side_effects=True, vmem_limit_bytes=60 * 1024 * 1024
@@ -385,7 +510,9 @@
 
     def program(queries, keys, values, doc_start):
         toks = queries.shape[2]
-        if 4 * toks == DOC_MAX and n_head * toks == 2 * DOC_MAX and queries.shape[0] % (2 * PIECE) == 0:
+        pieces = queries.shape[0] // (2 * PIECE)
+        fits = queries.shape[0] % (2 * PIECE) == 0 and 1 < n_ctx and (n_ctx - 1) * DETOUR <= pieces
+        if 4 * toks == DOC_MAX and n_head * toks == 2 * DOC_MAX and fits:
             return chunk_shards(n_ctx, n_head, queries, keys, values, doc_start)
         return shards(queries, keys, values, doc_start)
 

time: 84.9 us -> 81.5 us (0.960)
  Pallas kernels: 78.5 us -> 75.8 us
    pallas_call x1, Pallas kernels: 78.5 us -> 75.8 us  [chunk_shards(): pl.pallas_call(functools.partial(chunk_kernel, n_ctx, n_head), out_shape=...]
where the time goes in v3:
time: 81.5 us; the launch traced here: 80.9 us
  Pallas kernels  75.8 us (93%)
  local copies, waits for them, and re-layouts  4.44 us (5%)
    pallas_call x1, Pallas kernels, chunk_shards(): pl.pallas_call(functools.partial(chunk_kernel, n_ctx, n_head), out_shape=...  75.8 us
    unnamed x7, local copies, waits for them, and re-layouts  4.44 us

profile of v3, /device:TPU:1, one launch (start us, length us, event | category | flops | bytes accessed | tf_op | source)
XLA Modules:
  0.0 80.9 jit_solution(15574858706346933133)
XLA Ops:
  0.6 75.8 %shard_map.67 = (bf16[32,96,128]{2,1,0:T(8,128)(2,1)}, bf16[32,96,128]{2,1,0:T(8,128)(2,1)}, bf16[32,96,128]{2,1,0:T(8,128)(2,1)}) custom-call(bf16[32,96,128]{2,1,0:T(8,128)(2,1)} %q_ref.1, bf16[32,96,128]{2,1,0:T(8,128)(2,1)} %k_ref.1, bf16[32,96,128]{2,1,0:T(8,128)(2,1)} %v_ref.1, s32[1,128]{1,0:T(1,128)} %bitcast.1), custom_call_target="tpu_custom_call" | custom-call | flops 2415919104 | bytes 4718592 | tf_op jit(solution)/shard_map/pallas_call | solution.py:479
  76.4 0.0 copy-start.1
  76.4 2.1 %copy.10 = bf16[32,96,128]{2,1,0:T(8,128)(2,1)} copy(bf16[32,96,128]{2,1,0:T(8,128)(2,1)} %get-tuple-element.6) | data formatting | bytes 1572864
  78.6 0.0 copy-done.1
  78.6 0.0 copy-start
  78.6 0.9 %copy.11 = bf16[32,96,128]{2,1,0:T(8,128)(2,1)} copy(bf16[32,96,128]{2,1,0:T(8,128)(2,1)S(1)} %copy-done.1) | data formatting | bytes 1572864
  79.5 0.5 copy-done
  80.0 0.9 %copy.12 = bf16[32,96,128]{2,1,0:T(8,128)(2,1)} copy(bf16[32,96,128]{2,1,0:T(8,128)(2,1)S(1)} %copy-done) | data formatting | bytes 1572864
Async XLA Ops:
  76.4 2.1 %copy-start.1 = (bf16[32,96,128]{2,1,0:T(8,128)(2,1)S(1)}, bf16[32,96,128]{2,1,0:T(8,128)(2,1)}, u32[]{:S(2)}) copy-start(bf16[32,96,128]{2,1,0:T(8,128)(2,1)} %get-tuple-element.7) | copy-start | bytes 2359300
  78.6 1.4 %copy-start = (bf16[32,96,128]{2,1,0:T(8,128)(2,1)S(1)}, bf16[32,96,128]{2,1,0:T(8,128)(2,1)}, u32[]{:S(2)}) copy-start(bf16[32,96,128]{2,1,0:T(8,128)(2,1)} %get-tuple-element.8) | copy-start | bytes 2359300

commit v4 on v3

--- a/solution.py
+++ b/solution.py
@@ -9,8 +9,9 @@
 from jax.sharding import PartitionSpec as P
 
 DOC_MAX = 512
-PIECE = 2
-DETOUR = 2
+PIECE = 1
+STEP = 2
+DETOUR = 3
 MESH = pl.DeviceIdType.MESH
 
 
@@ -259,6 +260,9 @@
     def own_out(i, p):
         dst = (dq_ref, dk_ref, dv_ref)[i].at[span(core * half, p)]
         return pltpu.make_async_copy(staged(i, core, p), dst, loc_out.at[i, p])
+
+    def each_step(body):
+        lax.fori_loop(0, pieces // STEP, lambda t, carry: (body(t), carry)[1], 0)
 
     def each(body):
         lax.fori_loop(0, pieces, lambda p, carry: (body(p), carry)[1], 0)
@@ -362,16 +366,25 @@
             stage_kv[0, s, h] = grad_k[:, n * toks : (n + 1) * toks]
             stage_kv[1, s, h] = grad_v[:, n * toks : (n + 1) * toks]
 
-    def work(p, slots):
-        for i in range(3):
-            dst = qbuf.at[mate, span(0, p)] if i == 0 else kvbuf.at[i - 1, 2 + mate, span(0, p)]
-            src = (q_ref, k_ref, v_ref)[i].at[span(mate * half, p)]
-            remote(src, dst, in_s.at[i, p], in_r.at[i, p], mate_id).wait_recv()
-        for n in range(PIECE):
-            one_head(p * PIECE + n, slots)
-        for i in range(3):
-            mate_out(i, p).start()
-            own_out(i, p).start()
+    def work(t, slots):
+        for n in range(STEP):
+            p = t * STEP + n
+            for i in range(3):
+                dst = qbuf.at[mate, span(0, p)] if i == 0 else kvbuf.at[i - 1, 2 + mate, span(0, p)]
+                src = (q_ref, k_ref, v_ref)[i].at[span(mate * half, p)]
+                remote(src, dst, in_s.at[i, p], in_r.at[i, p], mate_id).wait_recv()
+        for n in range(STEP * PIECE):
+            one_head(t * STEP * PIECE + n, slots)
+        for n in range(STEP):
+            for i in range(3):
+                mate_out(i, t * STEP + n).start()
+                own_out(i, t * STEP + n).start()
+
+    def relay_step(t):
+        for n in range(STEP):
+            @pl.when(t * STEP + n < items)
+            def _():
+                relay(ahead_onward, t * STEP + n)
 
     @pl.when(is_right)
     def _():
@@ -380,48 +393,59 @@
                 for i in range(2):
                     back(i, j, p).start()
 
+        def send_detour(r):
+            for j in range(2):
+                for i in range(2):
+                    back_detour(i, j, r).start()
+
         def send_most():
-            for r in range(DETOUR):
+            @pl.when(jnp.logical_not(far))
+            def _():
+                for r in range(DETOUR):
+                    send_detour(r)
+
+            lax.fori_loop(DETOUR, pieces - STEP, lambda e, carry: (send_back(e), carry)[1], 0)
+
+        def step(t):
+            for n in range(STEP):
                 for j in range(2):
                     for i in range(2):
-                        back_detour(i, j, r).start()
-            lax.fori_loop(DETOUR, pieces - 1, lambda e, carry: (send_back(e), carry)[1], 0)
-
-        def step(p):
-            for j in range(2):
-                for i in range(2):
-                    ahead_arrival(i, j, p).wait_recv()
-
-            @pl.when(chained & (p == pieces - 1))
+                        ahead_arrival(i, j, t * STEP + n).wait_recv()
+
+            @pl.when(chained & (t == pieces // STEP - 1))
             def _():
                 send_most()
 
-            work(p, (0, 1, 2, 3))
+            work(t, (0, 1, 2, 3))
+
+            for n in range(STEP):
+                @pl.when(chained & far & (t * STEP + n < DETOUR))
+                def _():
+                    send_detour(t * STEP + n)
 
             @pl.when(jnp.logical_not(chained))
             def _():
-                send_back(p)
-
-                @pl.when(p < items)
-                def _():
-                    relay(ahead_onward, p)
-
-        each(step)
+                for n in range(STEP):
+                    send_back(t * STEP + n)
+                relay_step(t)
+
+        each_step(step)
 
         @pl.when(chained)
         def _():
-            send_back(pieces - 1)
+            for n in range(STEP):
+                send_back(pieces - STEP + n)
 
     @pl.when(jnp.logical_not(is_right))
     def _():
-        def step(p):
-            work(p, (2, 3))
-
-            @pl.when((chip == last) & (p < items))
+        def step(t):
+            work(t, (2, 3))
+
+            @pl.when(chip == last)
             def _():
-                relay(ahead_onward, p)
-
-        each(step)
+                relay_step(t)
+
+        each_step(step)
 
     def drain(p):
         for i in range(3):
@@ -511,7 +535,7 @@
     def program(queries, keys, values, doc_start):
         toks = queries.shape[2]
         pieces = queries.shape[0] // (2 * PIECE)
-        fits = queries.shape[0] % (2 * PIECE) == 0 and 1 < n_ctx and (n_ctx - 1) * DETOUR <= pieces
+        fits = queries.shape[0] % (2 * PIECE * STEP) == 0 and 1 < n_ctx and (n_ctx - 1) * DETOUR <= pieces - STEP
         if 4 * toks == DOC_MAX and n_head * toks == 2 * DOC_MAX and fits:
             return chunk_shards(n_ctx, n_head, queries, keys, values, doc_start)
         return shards(queries, keys, values, doc_start)

time: 81.5 us -> 81.3 us (level)
  no operation moved by 1% of the time
where the time goes in v4:
time: 81.3 us; the launch traced here: 81 us
  Pallas kernels  75.9 us (93%)
  local copies, waits for them, and re-layouts  4.44 us (5%)
    pallas_call x1, Pallas kernels, chunk_shards(): pl.pallas_call(functools.partial(chunk_kernel, n_ctx, n_head), out_shape=...  75.9 us
    unnamed x7, local copies, waits for them, and re-layouts  4.44 us

profile of v4, /device:TPU:1, one launch (start us, length us, event | category | flops | bytes accessed | tf_op | source)
XLA Modules:
  0.0 81.0 jit_solution(18394461976309931924)
XLA Ops:
  0.6 75.9 %shard_map.67 = (bf16[32,96,128]{2,1,0:T(8,128)(2,1)}, bf16[32,96,128]{2,1,0:T(8,128)(2,1)}, bf16[32,96,128]{2,1,0:T(8,128)(2,1)}) custom-call(bf16[32,96,128]{2,1,0:T(8,128)(2,1)} %q_ref.1, bf16[32,96,128]{2,1,0:T(8,128)(2,1)} %k_ref.1, bf16[32,96,128]{2,1,0:T(8,128)(2,1)} %v_ref.1, s32[1,128]{1,0:T(1,128)} %bitcast.1), custom_call_target="tpu_custom_call" | custom-call | flops 2415919104 | bytes 4718592 | tf_op jit(solution)/shard_map/pallas_call | solution.py:503
  76.6 0.0 copy-start.1
  76.6 2.1 %copy.10 = bf16[32,96,128]{2,1,0:T(8,128)(2,1)} copy(bf16[32,96,128]{2,1,0:T(8,128)(2,1)} %get-tuple-element.6) | data formatting | bytes 1572864
  78.7 0.0 copy-done.1
  78.7 0.0 copy-start
  78.7 0.9 %copy.11 = bf16[32,96,128]{2,1,0:T(8,128)(2,1)} copy(bf16[32,96,128]{2,1,0:T(8,128)(2,1)S(1)} %copy-done.1) | data formatting | bytes 1572864
  79.6 0.5 copy-done
  80.2 0.9 %copy.12 = bf16[32,96,128]{2,1,0:T(8,128)(2,1)} copy(bf16[32,96,128]{2,1,0:T(8,128)(2,1)S(1)} %copy-done) | data formatting | bytes 1572864
Async XLA Ops:
  76.6 2.1 %copy-start.1 = (bf16[32,96,128]{2,1,0:T(8,128)(2,1)S(1)}, bf16[32,96,128]{2,1,0:T(8,128)(2,1)}, u32[]{:S(2)}) copy-start(bf16[32,96,128]{2,1,0:T(8,128)(2,1)} %get-tuple-element.7) | copy-start | bytes 2359300
  78.7 1.4 %copy-start = (bf16[32,96,128]{2,1,0:T(8,128)(2,1)S(1)}, bf16[32,96,128]{2,1,0:T(8,128)(2,1)}, u32[]{:S(2)}) copy-start(bf16[32,96,128]{2,1,0:T(8,128)(2,1)} %get-tuple-element.8) | copy-start | bytes 2359300

commit v5 on v4

--- a/solution.py
+++ b/solution.py
@@ -341,30 +341,41 @@
     key_pos = base - wide + lax.broadcasted_iota(jnp.int32, (2 * wide, wide), 0)
     bias[...] = jnp.where((key_pos >= first) & (key_pos <= query_pos), 0.0, -jnp.inf)
 
-    def one_head(h, slots):
-        query = jnp.concatenate([qbuf[0, h], qbuf[1, h]], axis=1)
-        key = jnp.concatenate([kvbuf[0, s, h] for s in slots], axis=1)
-        value = jnp.concatenate([kvbuf[1, s, h] for s in slots], axis=1)
+    def some_heads(first_head, slots):
+        hs = [first_head + n for n in range(STEP * PIECE)]
         rows = pl.ds(slots[0] * toks, len(slots) * toks)
         dot = functools.partial(lax.dot_general, preferred_element_type=jnp.float32)
         tn, nn, nt = ((((0,), (0,)), ((), ())), (((1,), (0,)), ((), ())), (((1,), (1,)), ((), ())))
-        scores = dot(key, query, tn) * (scale * math.log2(math.e)) + bias[rows, :]
-        weights = jnp.exp2(scores - jnp.max(scores, axis=0, keepdims=True))
-        probs = weights * (1.0 / jnp.sum(weights, axis=0, keepdims=True))
-        low = probs.astype(jnp.bfloat16)
-        attended = dot(value, low, nn).astype(jnp.bfloat16)
-        wide_att = attended.astype(jnp.float32)
-        row_dot = jnp.sum(wide_att * wide_att, axis=0, keepdims=True)
-        grad_probs = dot(value, attended, tn)
-        grad_scores = (probs * (grad_probs - row_dot)).astype(jnp.bfloat16)
-        grad_q = (dot(key, grad_scores, nn) * scale).astype(jnp.bfloat16)
-        grad_k = (dot(query, grad_scores, nt) * scale).astype(jnp.bfloat16)
-        grad_v = dot(attended, low, nt).astype(jnp.bfloat16)
-        for j in range(2):
-            stage_q[j, h] = grad_q[:, j * toks : (j + 1) * toks]
-        for n, s in enumerate(slots):
-            stage_kv[0, s, h] = grad_k[:, n * toks : (n + 1) * toks]
-            stage_kv[1, s, h] = grad_v[:, n * toks : (n + 1) * toks]
+
+        def query(h):
+            return jnp.concatenate([qbuf[0, h], qbuf[1, h]], axis=1)
+
+        def window(i, h):
+            return jnp.concatenate([kvbuf[i, s, h] for s in slots], axis=1)
+
+        scores = [dot(window(0, h), query(h), tn) for h in hs]
+        probs, low, attended, grad_scores = [], [], [], []
+        for h, raw in zip(hs, scores):
+            raw = raw * (scale * math.log2(math.e)) + bias[rows, :]
+            weights = jnp.exp2(raw - jnp.max(raw, axis=0, keepdims=True))
+            probs.append(weights * (1.0 / jnp.sum(weights, axis=0, keepdims=True)))
+            low.append(probs[-1].astype(jnp.bfloat16))
+            attended.append(dot(window(1, h), low[-1], nn).astype(jnp.bfloat16))
+        grad_probs = [dot(window(1, h), att, tn) for h, att in zip(hs, attended)]
+        for n, h in enumerate(hs):
+            wide_att = attended[n].astype(jnp.float32)
+            row_dot = jnp.sum(wide_att * wide_att, axis=0, keepdims=True)
+            grad_scores.append((probs[n] * (grad_probs[n] - row_dot)).astype(jnp.bfloat16))
+            grad_v = dot(attended[n], low[n], nt).astype(jnp.bfloat16)
+            for m, s in enumerate(slots):
+                stage_kv[1, s, h] = grad_v[:, m * toks : (m + 1) * toks]
+        for n, h in enumerate(hs):
+            grad_q = (dot(window(0, h), grad_scores[n], nn) * scale).astype(jnp.bfloat16)
+            grad_k = (dot(query(h), grad_scores[n], nt) * scale).astype(jnp.bfloat16)
+            for j in range(2):
+                stage_q[j, h] = grad_q[:, j * toks : (j + 1) * toks]
+            for m, s in enumerate(slots):
+                stage_kv[0, s, h] = grad_k[:, m * toks : (m + 1) * toks]
 
     def work(t, slots):
         for n in range(STEP):
@@ -373,8 +384,7 @@
                 dst = qbuf.at[mate, span(0, p)] if i == 0 else kvbuf.at[i - 1, 2 + mate, span(0, p)]
                 src = (q_ref, k_ref, v_ref)[i].at[span(mate * half, p)]
                 remote(src, dst, in_s.at[i, p], in_r.at[i, p], mate_id).wait_recv()
-        for n in range(STEP * PIECE):
-            one_head(t * STEP * PIECE + n, slots)
+        some_heads(t * STEP * PIECE, slots)
         for n in range(STEP):
             for i in range(3):
                 mate_out(i, t * STEP + n).start()
@@ -404,7 +414,7 @@
                 for r in range(DETOUR):
                     send_detour(r)
 
-            lax.fori_loop(DETOUR, pieces - STEP, lambda e, carry: (send_back(e), carry)[1], 0)
+            lax.fori_loop(DETOUR, pieces - 2 * STEP, lambda e, carry: (send_back(e), carry)[1], 0)
 
         def step(t):
             for n in range(STEP):
@@ -412,7 +422,7 @@
                     for i in range(2):
                         ahead_arrival(i, j, t * STEP + n).wait_recv()
 
-            @pl.when(chained & (t == pieces // STEP - 1))
+            @pl.when(chained & (t == pieces // STEP - 2))
             def _():
                 send_most()
 
@@ -423,18 +433,16 @@
                 def _():
                     send_detour(t * STEP + n)
 
-            @pl.when(jnp.logical_not(chained))
+            @pl.when(jnp.logical_not(chained) | (t >= pieces // STEP - 2))
             def _():
                 for n in range(STEP):
                     send_back(t * STEP + n)
+
+            @pl.when(jnp.logical_not(chained))
+            def _():
                 relay_step(t)
 
         each_step(step)
-
-        @pl.when(chained)
-        def _():
-            for n in range(STEP):
-                send_back(pieces - STEP + n)
 
     @pl.when(jnp.logical_not(is_right))
     def _():
@@ -535,7 +543,7 @@
     def program(queries, keys, values, doc_start):
         toks = queries.shape[2]
         pieces = queries.shape[0] // (2 * PIECE)
-        fits = queries.shape[0] % (2 * PIECE * STEP) == 0 and 1 < n_ctx and (n_ctx - 1) * DETOUR <= pieces - STEP
+        fits = queries.shape[0] % (2 * PIECE * STEP) == 0 and 1 < n_ctx and (n_ctx - 1) * DETOUR <= pieces - 2 * STEP
         if 4 * toks == DOC_MAX and n_head * toks == 2 * DOC_MAX and fits:
             return chunk_shards(n_ctx, n_head, queries, keys, values, doc_start)
         return shards(queries, keys, values, doc_start)

time: 81.3 us -> 81.3 us (level)
  no operation moved by 1% of the time
where the time goes in v5:
time: 81.3 us; the launch traced here: 81 us
  Pallas kernels  75.9 us (93%)
  local copies, waits for them, and re-layouts  4.44 us (5%)
    pallas_call x1, Pallas kernels, chunk_shards(): pl.pallas_call(functools.partial(chunk_kernel, n_ctx, n_head), out_shape=...  75.9 us
    unnamed x7, local copies, waits for them, and re-layouts  4.44 us

profile of v5, /device:TPU:1, one launch (start us, length us, event | category | flops | bytes accessed | tf_op | source)
XLA Modules:
  0.0 81.0 jit_solution(8613081315589203247)
XLA Ops:
  0.6 75.9 %shard_map.67 = (bf16[32,96,128]{2,1,0:T(8,128)(2,1)}, bf16[32,96,128]{2,1,0:T(8,128)(2,1)}, bf16[32,96,128]{2,1,0:T(8,128)(2,1)}) custom-call(bf16[32,96,128]{2,1,0:T(8,128)(2,1)} %q_ref.1, bf16[32,96,128]{2,1,0:T(8,128)(2,1)} %k_ref.1, bf16[32,96,128]{2,1,0:T(8,128)(2,1)} %v_ref.1, s32[1,128]{1,0:T(1,128)} %bitcast.1), custom_call_target="tpu_custom_call" | custom-call | flops 2415919104 | bytes 4718592 | tf_op jit(solution)/shard_map/pallas_call | solution.py:511
  76.6 0.0 copy-start.1
  76.6 2.1 %copy.10 = bf16[32,96,128]{2,1,0:T(8,128)(2,1)} copy(bf16[32,96,128]{2,1,0:T(8,128)(2,1)} %get-tuple-element.6) | data formatting | bytes 1572864
  78.7 0.0 copy-done.1
  78.7 0.0 copy-start
  78.7 0.9 %copy.11 = bf16[32,96,128]{2,1,0:T(8,128)(2,1)} copy(bf16[32,96,128]{2,1,0:T(8,128)(2,1)S(1)} %copy-done.1) | data formatting | bytes 1572864
  79.6 0.5 copy-done
  80.2 0.9 %copy.12 = bf16[32,96,128]{2,1,0:T(8,128)(2,1)} copy(bf16[32,96,128]{2,1,0:T(8,128)(2,1)S(1)} %copy-done) | data formatting | bytes 1572864
Async XLA Ops:
  76.6 2.1 %copy-start.1 = (bf16[32,96,128]{2,1,0:T(8,128)(2,1)S(1)}, bf16[32,96,128]{2,1,0:T(8,128)(2,1)}, u32[]{:S(2)}) copy-start(bf16[32,96,128]{2,1,0:T(8,128)(2,1)} %get-tuple-element.7) | copy-start | bytes 2359300
  78.7 1.4 %copy-start = (bf16[32,96,128]{2,1,0:T(8,128)(2,1)S(1)}, bf16[32,96,128]{2,1,0:T(8,128)(2,1)}, u32[]{:S(2)}) copy-start(bf16[32,96,128]{2,1,0:T(8,128)(2,1)} %get-tuple-element.8) | copy-start | bytes 2359300

commit v6 on v5

--- a/solution.py
+++ b/solution.py
@@ -464,9 +464,22 @@
 
     each(drain)
 
+    def ahead_sent(p):
+        for j in range(2):
+            for i in range(2):
+                ahead(i, j, p).wait_send()
+
+    @pl.when(is_left & relays_back)
+    def _():
+        each(ahead_sent)
+
     @pl.when(relays_back)
     def _():
         lax.fori_loop(0, items, lambda t, carry: (relay(back_onward, t), carry)[1], 0)
+
+    @pl.when(is_left & jnp.logical_not(relays_back))
+    def _():
+        each(ahead_sent)
 
     @pl.when(is_left)
     def _():
@@ -474,7 +487,6 @@
             for i in range(2):
                 out = (dk_ref, dv_ref)[i]
                 for j in range(2):
-                    ahead(i, j, p).wait_send()
                     back_arrival(i, j, p).wait_recv()
                     at = span(j * half, p)
                     total = out[at].astype(jnp.float32) + part[i, j, span(0, p)].astype(jnp.float32)

time: 81.3 us -> 81.3 us (level)
  no operation moved by 1% of the time
where the time goes in v6:
time: 81.3 us; the launch traced here: 81 us
  Pallas kernels  75.9 us (93%)
  local copies, waits for them, and re-layouts  4.44 us (5%)
    pallas_call x1, Pallas kernels, chunk_shards(): pl.pallas_call(functools.partial(chunk_kernel, n_ctx, n_head), out_shape=...  75.9 us
    unnamed x7, local copies, waits for them, and re-layouts  4.44 us

profile of v6, /device:TPU:1, one launch (start us, length us, event | category | flops | bytes accessed | tf_op | source)
XLA Modules:
  0.0 81.0 jit_solution(16732152630539470149)
XLA Ops:
  0.6 75.9 %shard_map.67 = (bf16[32,96,128]{2,1,0:T(8,128)(2,1)}, bf16[32,96,128]{2,1,0:T(8,128)(2,1)}, bf16[32,96,128]{2,1,0:T(8,128)(2,1)}) custom-call(bf16[32,96,128]{2,1,0:T(8,128)(2,1)} %q_ref.1, bf16[32,96,128]{2,1,0:T(8,128)(2,1)} %k_ref.1, bf16[32,96,128]{2,1,0:T(8,128)(2,1)} %v_ref.1, s32[1,128]{1,0:T(1,128)} %bitcast.1), custom_call_target="tpu_custom_call" | custom-call | flops 2415919104 | bytes 4718592 | tf_op jit(solution)/shard_map/pallas_call | solution.py:523
  76.6 0.0 copy-start.1
  76.6 2.1 %copy.10 = bf16[32,96,128]{2,1,0:T(8,128)(2,1)} copy(bf16[32,96,128]{2,1,0:T(8,128)(2,1)} %get-tuple-element.6) | data formatting | bytes 1572864
  78.7 0.0 copy-done.1
  78.7 0.0 copy-start
  78.7 0.9 %copy.11 = bf16[32,96,128]{2,1,0:T(8,128)(2,1)} copy(bf16[32,96,128]{2,1,0:T(8,128)(2,1)S(1)} %copy-done.1) | data formatting | bytes 1572864
  79.6 0.5 copy-done
  80.2 0.9 %copy.12 = bf16[32,96,128]{2,1,0:T(8,128)(2,1)} copy(bf16[32,96,128]{2,1,0:T(8,128)(2,1)S(1)} %copy-done) | data formatting | bytes 1572864
Async XLA Ops:
  76.6 2.1 %copy-start.1 = (bf16[32,96,128]{2,1,0:T(8,128)(2,1)S(1)}, bf16[32,96,128]{2,1,0:T(8,128)(2,1)}, u32[]{:S(2)}) copy-start(bf16[32,96,128]{2,1,0:T(8,128)(2,1)} %get-tuple-element.7) | copy-start | bytes 2359300
  78.7 1.4 %copy-start = (bf16[32,96,128]{2,1,0:T(8,128)(2,1)S(1)}, bf16[32,96,128]{2,1,0:T(8,128)(2,1)}, u32[]{:S(2)}) copy-start(bf16[32,96,128]{2,1,0:T(8,128)(2,1)} %get-tuple-element.8) | copy-start | bytes 2359300
